TPU v7x, 512 devices: a whole 4x8x8 slice. The times are simulated.
512 devices in a mesh: lat: 16 (over x_lo, z), lon: 32 (over x_hi, y, core).
Axes of the slice: x: 4 (x_hi: 2, x_lo: 2; x = x_hi * 2 + x_lo), y: 8, z: 8, core: 2. Of those that a mesh axis runs over, the one named last changes fastest.
Arguments:
- fields: bfloat16 [75, 128, 4096], P(None, 'lat', 'lon'), may hold values from -6 to 6
- mask: int32 [128, 4096], P('lat', 'lon'), may hold values from 0 to 1, as said below
- w1: bfloat16 [9, 48, 75], replicated, may hold values from -0.25 to 0.25
- w2: bfloat16 [9, 48, 48], replicated, may hold values from -0.3125 to 0.3125
- cotangent: bfloat16 [48, 128, 4096], P(None, 'lat', 'lon'), may hold values from -6 to 6
Outputs:
- output: bfloat16 [48, 128, 4096], P(None, 'lat', 'lon')
- dx: bfloat16 [75, 128, 4096], P(None, 'lat', 'lon')
- dw1: float32 [9, 48, 75], replicated
- dw2: float32 [9, 48, 48], replicated
Inputs may be any that keep to these rules, and one draw needn't show every extreme that they name: `mask`: rows below 8 are sea. Each aligned block of 8 x 8 grid points is all land or all sea.
All inputs are finite; a program needn't handle non-finite values.
Results may differ from a plain program's by a relative error of at most 0.017.
Values may be sent and summed in bfloat16 or wider, within the bound.
A program may use at most 64 MiB of HBM per device.

v0:
```python
import math
import jax
import jax.numpy as jnp
from jax import lax
from jax.sharding import PartitionSpec as P


def from_partner(x, axis, bit):
    return lax.ppermute(x, axis, [(i, i ^ 1 << bit) for i in range(lax.axis_size(axis))])


def extended(x, sides, width, wrap):
    for axis, dim in sides:
        peers, length = (lax.axis_size(axis), x.shape[dim])
        up = [(i, (i + 1) % peers) for i in range(peers if wrap else peers - 1)]
        down = [(j, i) for i, j in up]
        last = lax.slice_in_dim(x, length - width, length, axis=dim)
        leading = lax.slice_in_dim(x, 0, width, axis=dim)
        before = lax.ppermute(last, axis, up)
        after = lax.ppermute(leading, axis, down)
        x = jnp.concatenate([before, x, after], axis=dim)
    return x


def gelu_parts(a):
    coeff = 0.7978845608
    inner = coeff * (a + 0.044715 * a * a * a)
    tval = jnp.tanh(inner)
    value = 0.5 * a * (1.0 + tval)
    slope = 0.5 * (1.0 + tval) + 0.5 * a * (1.0 - tval * tval) * coeff * (1.0 + 0.134145 * a * a)
    return (value, slope)


def at_top():
    return lax.axis_index("lat") == lax.axis_size("lat") - 1


def bit_order():
    count = lax.axis_size("lon").bit_length() - 1
    return list(range(count))


def mirror_fwd(row_top):
    moved = row_top
    for bitnum in bit_order():
        moved = from_partner(moved, "lon", bitnum)
    return moved[:, ::-1]


def mirror_back(row_top):
    moved = row_top
    for bitnum in bit_order():
        moved = from_partner(moved.astype(jnp.bfloat16), "lon", bitnum).astype(moved.dtype)
    return moved[:, ::-1]


def extend(field):
    rows_ext = extended(field, (("lat", 1),), 1, False)
    folded = mirror_fwd(field[:, -1, :])
    top_row = jnp.where(at_top(), folded, rows_ext[:, -1, :])
    rows_ext = jnp.concatenate([rows_ext[:, :-1, :], top_row[:, None, :]], axis=1)
    return extended(rows_ext, (("lon", 2),), 1, True)


def retract(padded):
    edges = jnp.stack((padded[:, :, 0], padded[:, :, -1]), 0)
    edge_got = extended(edges, (("lon", 0),), 1, True)
    inner = padded[:, :, 1:-1]
    inner = inner.at[:, :, 0].add(edge_got[0]).at[:, :, -1].add(edge_got[3])
    rims = jnp.stack((inner[:, 0, :], inner[:, -1, :]), 0)
    rim_got = extended(rims.astype(jnp.bfloat16), (("lat", 0),), 1, False).astype(rims.dtype)
    folded = mirror_back(inner[:, -1, :])
    result = inner[:, 1:-1, :]
    top_add = rim_got[3] + jnp.where(at_top(), folded, 0.0)
    return result.at[:, 0, :].add(rim_got[0]).at[:, -1, :].add(top_add)


def conv(padded, kernel):
    rows_n = padded.shape[1] - 2
    cols_n = padded.shape[2] - 2
    total = jnp.zeros((kernel.shape[1], rows_n, cols_n), jnp.float32)
    for tap in range(9):
        drow, dcol = (tap // 3, tap % 3)
        total = total + jnp.einsum(
            "oi,ihw->ohw",
            kernel[tap],
            padded[:, drow : drow + rows_n, dcol : dcol + cols_n],
            preferred_element_type=jnp.float32,
        )
    return total


def tconv(grad, kernel):
    rows_n = grad.shape[1]
    cols_n = grad.shape[2]
    wide = jnp.pad(grad, ((0, 0), (2, 2), (2, 2)))
    total = jnp.zeros((kernel.shape[2], rows_n + 2, cols_n + 2), jnp.float32)
    for tap in range(9):
        drow, dcol = (tap // 3, tap % 3)
        total = total + jnp.einsum(
            "oi,ohw->ihw",
            kernel[tap],
            wide[:, 2 - drow : 4 - drow + rows_n, 2 - dcol : 4 - dcol + cols_n],
            preferred_element_type=jnp.float32,
        )
    return total


def wgrad(grad, padded):
    rows_n = grad.shape[1]
    cols_n = grad.shape[2]
    terms = []
    for tap in range(9):
        drow, dcol = (tap // 3, tap % 3)
        terms.append(
            jnp.einsum(
                "ohw,ihw->oi",
                grad,
                padded[:, drow : drow + rows_n, dcol : dcol + cols_n],
                preferred_element_type=jnp.float32,
            )
        )
    return jnp.stack(terms, 0)


def body(fields, mask, w1, w2, cotangent):
    sea = mask.astype(jnp.float32)
    x_ext = extend(fields)
    value, slope = gelu_parts(conv(x_ext, w1))
    hidden = (value * sea).astype(jnp.bfloat16)
    gate = slope * sea
    h_ext = extend(hidden)
    out_block = (conv(h_ext, w2) * sea).astype(jnp.bfloat16)
    grad_out = cotangent * mask.astype(jnp.bfloat16)
    term_w2 = wgrad(grad_out, h_ext)
    grad_h_ext = tconv(grad_out, w2)
    grad_h = retract(grad_h_ext)
    grad_a = (grad_h * gate).astype(jnp.bfloat16)
    term_w1 = wgrad(grad_a, x_ext)
    grad_x_ext = tconv(grad_a, w1)
    dx = retract(grad_x_ext).astype(jnp.bfloat16)
    grad_w1, grad_w2 = lax.psum((term_w1, term_w2), ("lat", "lon"))
    cells = fields.shape[1] * fields.shape[2] * lax.axis_size("lat") * lax.axis_size("lon")
    factor = 1.0 / math.sqrt(cells)
    return (out_block, dx, grad_w1 * factor, grad_w2 * factor)


def solution(mesh):
    in_specs = (P(None, "lat", "lon"), P("lat", "lon"), P(), P(), P(None, "lat", "lon"))
    out_specs = (P(None, "lat", "lon"), P(None, "lat", "lon"), P(), P())
    return jax.shard_map(body, mesh=mesh, in_specs=in_specs, out_specs=out_specs, check_vma=False)
```

profile of v0, /device:TPU:1, one launch (start us, length us, event | category | flops | bytes accessed | tf_op | source)
XLA Modules:
  0.0 454.7 jit_solution(2405748562817227738)
XLA Ops:
  11.8 4.6 %collective-permute-start.18 = (f32[1,48,10]{1,0,2:T(1,128)S(1)}, f32[1,48,10]{1,0,2:T(1,128)S(1)}, u32[]{:S(2)}, u32[]{:S(2)}) collective-permute-start(f32[1,48,10]{1,0,2:T(1,128)S(1)} %stack_squeeze.28), channel_id=1, source_target_pairs={{0,1},{1,2},{2,3},{3,4},{4,5},{5,6},{6,7},{7,8},{8,9},{9,10},{10,1... | collective-permute-start | bytes 5768 | tf_op jit(solution)/shard_map/ppermute | solution.py:19
  16.4 6.1 %collective-permute-start.19 = (f32[1,48,10]{1,0,2:T(1,128)S(1)}, f32[1,48,10]{1,0,2:T(1,128)S(1)}, u32[]{:S(2)}, u32[]{:S(2)}) collective-permute-start(f32[1,48,10]{1,0,2:T(1,128)S(1)} %stack_squeeze.29), channel_id=1, source_target_pairs={{1,0},{2,1},{3,2},{4,3},{5,4},{6,5},{7,6},{8,7},{9,8},{10,9},{11,1... | collective-permute-start | bytes 5768 | tf_op jit(solution)/shard_map/ppermute | solution.py:20
  22.7 7.3 %collective-permute-start.1 = (bf16[75,128]{0,1:T(8,128)(2,1)S(1)}, bf16[75,128]{0,1:T(8,128)(2,1)S(1)}, u32[]{:S(2)}, u32[]{:S(2)}) collective-permute-start(bf16[75,128]{0,1:T(8,128)(2,1)S(1)} %bitcast.327), channel_id=1, source_target_pairs={{0,1},{1,0},{2,3},{3,2},{4,5},{5,4},{6,7},{7,6},{8,9},{9,8},{10,11... | collective-permute-start | bytes 57608 | tf_op jit(solution)/shard_map/ppermute | solution.py:9
  36.9 3.4 collective-permute-start.23
  43.5 4.3 collective-permute-start.24
  47.8 4.0 collective-permute-start.20
  55.4 2.8 collective-permute-start.25
  58.1 6.4 %collective-permute-start.4 = (bf16[75,128]{0,1:T(8,128)(2,1)S(1)}, bf16[75,128]{0,1:T(8,128)(2,1)S(1)}, u32[]{:S(2)}, u32[]{:S(2)}) collective-permute-start(bf16[75,128]{0,1:T(8,128)(2,1)S(1)} %collective-permute-done.3), channel_id=1, source_target_pairs={{0,8},{1,9},{2,10},{3,11},{4,12},{5,13},{6,14},{7,15},{8,0},{9,1},... | collective-permute-start | bytes 57608 | tf_op jit(solution)/shard_map/ppermute | solution.py:9
  66.9 4.8 %collective-permute-start.5 = (bf16[75,128]{0,1:T(8,128)(2,1)S(1)}, bf16[75,128]{0,1:T(8,128)(2,1)S(1)}, u32[]{:S(2)}, u32[]{:S(2)}) collective-permute-start(bf16[75,128]{0,1:T(8,128)(2,1)S(1)} %collective-permute-done.4), channel_id=1, source_target_pairs={{0,16},{1,17},{2,18},{3,19},{4,20},{5,21},{6,22},{7,23},{8,24},{9,... | collective-permute-start | bytes 57608 | tf_op jit(solution)/shard_map/ppermute | solution.py:9
  73.4 6.0 %collective-permute-start.8 = (bf16[75,10,1]{2,0,1:T(8,128)(2,1)S(1)}, bf16[75,10,1]{2,0,1:T(8,128)(2,1)S(1)}, u32[]{:S(2)}, u32[]{:S(2)}) collective-permute-start(bf16[75,10,1]{2,0,1:T(8,128)(2,1)S(1)} %get-tuple-element.134), channel_id=1, source_target_pairs={{1,0},{2,1},{3,2},{4,3},{5,4},{6,5},{7,6},{8,7},{9,8},{10,9},{11,1... | collective-permute-start | bytes 4508 | tf_op jit(solution)/shard_map/ppermute | solution.py:20
  79.5 3.1 collective-permute-start.7
  88.0 4.5 collective-permute-start.9
  92.5 7.7 %collective-permute-start.10 = (bf16[48,128]{1,0:T(8,128)(2,1)S(1)}, bf16[48,128]{1,0:T(8,128)(2,1)S(1)}, u32[]{:S(2)}, u32[]{:S(2)}) collective-permute-start(bf16[48,128]{1,0:T(8,128)(2,1)S(1)} %get-tuple-element.145), channel_id=1, source_target_pairs={{0,1},{1,0},{2,3},{3,2},{4,5},{5,4},{6,7},{7,6},{8,9},{9,8},{10,11... | collective-permute-start | bytes 36872 | tf_op jit(solution)/shard_map/ppermute | solution.py:9
  111.3 2.7 collective-permute-done.28
  116.1 5.3 %collective-permute-start.31 = (bf16[75,128]{0,1:T(8,128)(2,1)S(1)}, bf16[75,128]{0,1:T(8,128)(2,1)S(1)}, u32[]{:S(2)}, u32[]{:S(2)}) collective-permute-start(bf16[75,128]{0,1:T(8,128)(2,1)S(1)} %get-tuple-element.126), channel_id=1, source_target_pairs={{0,1},{1,0},{2,3},{3,2},{4,5},{5,4},{6,7},{7,6},{8,9},{9,8},{10,11... | collective-permute-start | bytes 57608 | tf_op jit(solution)/shard_map/ppermute | solution.py:9
  125.5 6.1 %collective-permute-start.29 = (bf16[1,75,128]{1,2,0:T(8,128)(2,1)S(1)}, bf16[1,75,128]{1,2,0:T(8,128)(2,1)S(1)}, u32[]{:S(2)}, u32[]{:S(2)}) collective-permute-start(bf16[1,75,128]{1,2,0:T(8,128)(2,1)S(1)} %get-tuple-element.128), channel_id=1, source_target_pairs={{0,32},{32,64},{64,96},{96,128},{128,160},{160,192},{192,224},{224... | collective-permute-start | bytes 57608 | tf_op jit(solution)/shard_map/ppermute | solution.py:19
  131.6 3.6 collective-permute-start.32
  135.3 8.4 %collective-permute-start.13 = (bf16[48,128]{1,0:T(8,128)(2,1)S(1)}, bf16[48,128]{1,0:T(8,128)(2,1)S(1)}, u32[]{:S(2)}, u32[]{:S(2)}) collective-permute-start(bf16[48,128]{1,0:T(8,128)(2,1)S(1)} %collective-permute-done.12), channel_id=1, source_target_pairs={{0,8},{1,9},{2,10},{3,11},{4,12},{5,13},{6,14},{7,15},{8,0},{9,1},... | collective-permute-start | bytes 36872 | tf_op jit(solution)/shard_map/ppermute | solution.py:9
  145.8 2.7 collective-permute-start.14
  149.4 5.3 %collective-permute-start.34 = (bf16[75,128]{0,1:T(8,128)(2,1)S(1)}, bf16[75,128]{0,1:T(8,128)(2,1)S(1)}, u32[]{:S(2)}, u32[]{:S(2)}) collective-permute-start(bf16[75,128]{0,1:T(8,128)(2,1)S(1)} %collective-permute-done.33), channel_id=1, source_target_pairs={{0,8},{1,9},{2,10},{3,11},{4,12},{5,13},{6,14},{7,15},{8,0},{9,1},... | collective-permute-start | bytes 57608 | tf_op jit(solution)/shard_map/ppermute | solution.py:9
  155.0 4.4 collective-permute-start.17
  159.4 3.3 collective-permute-start.16
  167.4 4.1 collective-permute-start.35
  174.5 271.0 %all-reduce.5.cloned.1.call-done = (f32[9,48,75]{2,1,0:T(8,128)}, f32[9,48,48]{2,1,0:T(8,128)}) async-done(((f32[9,48,75]{2,1,0:T(8,128)}, f32[9,48,48]{2,1,0:T(8,128)}), (f32[9,48,75]{2,1,0:T(8,128)}, f32[9,48,48]{2,1,0:T(8,128)})) %all-reduce.5.cloned.1.call-update) | async-done | bytes 212560 | tf_op jit(solution)/shard_map/psum | solution.py:142
  (167 shorter events, 57.6 us)
Async XLA Ops:
  7.2 438.3 %all-reduce.5.cloned.1.call-start = ((), (), s32[]{:S(2)}) async-start(), calls=%async_computation | async-start | bytes 884736 | tf_op jit(solution)/shard_map/psum | solution.py:142
  11.8 18.5 %collective-permute-start.18 = (f32[1,48,10]{1,0,2:T(1,128)S(1)}, f32[1,48,10]{1,0,2:T(1,128)S(1)}, u32[]{:S(2)}, u32[]{:S(2)}) collective-permute-start(f32[1,48,10]{1,0,2:T(1,128)S(1)} %stack_squeeze.28), channel_id=1, source_target_pairs={{0,1},{1,2},{2,3},{3,4},{4,5},{5,6},{6,7},{7,8},{8,9},{9,10},{10,1... | collective-permute-start | bytes 5768 | tf_op jit(solution)/shard_map/ppermute | solution.py:19
  16.4 13.7 %collective-permute-start.19 = (f32[1,48,10]{1,0,2:T(1,128)S(1)}, f32[1,48,10]{1,0,2:T(1,128)S(1)}, u32[]{:S(2)}, u32[]{:S(2)}) collective-permute-start(f32[1,48,10]{1,0,2:T(1,128)S(1)} %stack_squeeze.29), channel_id=1, source_target_pairs={{1,0},{2,1},{3,2},{4,3},{5,4},{6,5},{7,6},{8,7},{9,8},{10,9},{11,1... | collective-permute-start | bytes 5768 | tf_op jit(solution)/shard_map/ppermute | solution.py:20
  22.7 9.2 %collective-permute-start.1 = (bf16[75,128]{0,1:T(8,128)(2,1)S(1)}, bf16[75,128]{0,1:T(8,128)(2,1)S(1)}, u32[]{:S(2)}, u32[]{:S(2)}) collective-permute-start(bf16[75,128]{0,1:T(8,128)(2,1)S(1)} %bitcast.327), channel_id=1, source_target_pairs={{0,1},{1,0},{2,3},{3,2},{4,5},{5,4},{6,7},{7,6},{8,9},{9,8},{10,11... | collective-permute-start | bytes 57608 | tf_op jit(solution)/shard_map/ppermute | solution.py:9
  40.3 17.9 %collective-permute-start.3 = (bf16[75,128]{0,1:T(8,128)(2,1)S(1)}, bf16[75,128]{0,1:T(8,128)(2,1)S(1)}, u32[]{:S(2)}, u32[]{:S(2)}) collective-permute-start(bf16[75,128]{0,1:T(8,128)(2,1)S(1)} %collective-permute-done.2), channel_id=1, source_target_pairs={{0,4},{1,5},{2,6},{3,7},{4,0},{5,1},{6,2},{7,3},{8,12},{9,13},{10,... | collective-permute-start | bytes 57608 | tf_op jit(solution)/shard_map/ppermute | solution.py:9
  42.2 11.7 %collective-permute-start.21 = (bf16[1,48,128]{2,1,0:T(8,128)(2,1)S(1)}, bf16[1,48,128]{2,1,0:T(8,128)(2,1)S(1)}, u32[]{:S(2)}, u32[]{:S(2)}) collective-permute-start(bf16[1,48,128]{2,1,0:T(8,128)(2,1)S(1)} %get-tuple-element.130), channel_id=1, source_target_pairs={{32,0},{64,32},{96,64},{128,96},{160,128},{192,160},{224,192},{256... | collective-permute-start | bytes 36872 | tf_op jit(solution)/shard_map/ppermute | solution.py:20
  43.5 11.8 %collective-permute-start.24 = (bf16[48,128]{1,0:T(8,128)(2,1)S(1)}, bf16[48,128]{1,0:T(8,128)(2,1)S(1)}, u32[]{:S(2)}, u32[]{:S(2)}) collective-permute-start(bf16[48,128]{1,0:T(8,128)(2,1)S(1)} %collective-permute-done.23), channel_id=1, source_target_pairs={{0,4},{1,5},{2,6},{3,7},{4,0},{5,1},{6,2},{7,3},{8,12},{9,13},{10,... | collective-permute-start | bytes 36872 | tf_op jit(solution)/shard_map/ppermute | solution.py:9
  47.8 16.8 %collective-permute-start.20 = (bf16[1,48,128]{2,1,0:T(8,128)(2,1)S(1)}, bf16[1,48,128]{2,1,0:T(8,128)(2,1)S(1)}, u32[]{:S(2)}, u32[]{:S(2)}) collective-permute-start(bf16[1,48,128]{2,1,0:T(8,128)(2,1)S(1)} %get-tuple-element.131), channel_id=1, source_target_pairs={{0,32},{32,64},{64,96},{96,128},{128,160},{160,192},{192,224},{224... | collective-permute-start | bytes 36872 | tf_op jit(solution)/shard_map/ppermute | solution.py:19
  51.8 12.8 %collective-permute-start = (bf16[75,1,128]{0,2,1:T(8,128)(2,1)S(1)}, bf16[75,1,128]{0,2,1:T(8,128)(2,1)S(1)}, u32[]{:S(2)}, u32[]{:S(2)}) collective-permute-start(bf16[75,1,128]{0,2,1:T(8,128)(2,1)S(1)} %copy.200), channel_id=1, source_target_pairs={{0,32},{32,64},{64,96},{96,128},{128,160},{160,192},{192,224},{224... | collective-permute-start | bytes 57608 | tf_op jit(solution)/shard_map/ppermute | solution.py:19
  53.9 19.2 %collective-permute-start.6 = (bf16[75,1,128]{0,2,1:T(8,128)(2,1)S(1)}, bf16[75,1,128]{0,2,1:T(8,128)(2,1)S(1)}, u32[]{:S(2)}, u32[]{:S(2)}) collective-permute-start(bf16[75,1,128]{0,2,1:T(8,128)(2,1)S(1)} %copy.201), channel_id=1, source_target_pairs={{32,0},{64,32},{96,64},{128,96},{160,128},{192,160},{224,192},{256... | collective-permute-start | bytes 57608 | tf_op jit(solution)/shard_map/ppermute | solution.py:20
  55.4 9.4 %collective-permute-start.25 = (bf16[48,128]{1,0:T(8,128)(2,1)S(1)}, bf16[48,128]{1,0:T(8,128)(2,1)S(1)}, u32[]{:S(2)}, u32[]{:S(2)}) collective-permute-start(bf16[48,128]{1,0:T(8,128)(2,1)S(1)} %collective-permute-done.24), channel_id=1, source_target_pairs={{0,8},{1,9},{2,10},{3,11},{4,12},{5,13},{6,14},{7,15},{8,0},{9,1},... | collective-permute-start | bytes 36872 | tf_op jit(solution)/shard_map/ppermute | solution.py:9
  58.1 8.8 %collective-permute-start.4 = (bf16[75,128]{0,1:T(8,128)(2,1)S(1)}, bf16[75,128]{0,1:T(8,128)(2,1)S(1)}, u32[]{:S(2)}, u32[]{:S(2)}) collective-permute-start(bf16[75,128]{0,1:T(8,128)(2,1)S(1)} %collective-permute-done.3), channel_id=1, source_target_pairs={{0,8},{1,9},{2,10},{3,11},{4,12},{5,13},{6,14},{7,15},{8,0},{9,1},... | collective-permute-start | bytes 57608 | tf_op jit(solution)/shard_map/ppermute | solution.py:9
  73.4 10.7 %collective-permute-start.8 = (bf16[75,10,1]{2,0,1:T(8,128)(2,1)S(1)}, bf16[75,10,1]{2,0,1:T(8,128)(2,1)S(1)}, u32[]{:S(2)}, u32[]{:S(2)}) collective-permute-start(bf16[75,10,1]{2,0,1:T(8,128)(2,1)S(1)} %get-tuple-element.134), channel_id=1, source_target_pairs={{1,0},{2,1},{3,2},{4,3},{5,4},{6,5},{7,6},{8,7},{9,8},{10,9},{11,1... | collective-permute-start | bytes 4508 | tf_op jit(solution)/shard_map/ppermute | solution.py:20
  88.0 37.5 %collective-permute-start.9 = (bf16[48,1,128]{2,0,1:T(8,128)(2,1)S(1)}, bf16[48,1,128]{2,0,1:T(8,128)(2,1)S(1)}, u32[]{:S(2)}, u32[]{:S(2)}) collective-permute-start(bf16[48,1,128]{2,0,1:T(8,128)(2,1)S(1)} %get-tuple-element.144), channel_id=1, source_target_pairs={{0,32},{32,64},{64,96},{96,128},{128,160},{160,192},{192,224},{224... | collective-permute-start | bytes 36872 | tf_op jit(solution)/shard_map/ppermute | solution.py:19
  92.5 21.6 %collective-permute-start.10 = (bf16[48,128]{1,0:T(8,128)(2,1)S(1)}, bf16[48,128]{1,0:T(8,128)(2,1)S(1)}, u32[]{:S(2)}, u32[]{:S(2)}) collective-permute-start(bf16[48,128]{1,0:T(8,128)(2,1)S(1)} %get-tuple-element.145), channel_id=1, source_target_pairs={{0,1},{1,0},{2,3},{3,2},{4,5},{5,4},{6,7},{7,6},{8,9},{9,8},{10,11... | collective-permute-start | bytes 36872 | tf_op jit(solution)/shard_map/ppermute | solution.py:9
  100.2 54.6 %collective-permute-start.15 = (bf16[48,1,128]{2,0,1:T(8,128)(2,1)S(1)}, bf16[48,1,128]{2,0,1:T(8,128)(2,1)S(1)}, u32[]{:S(2)}, u32[]{:S(2)}) collective-permute-start(bf16[48,1,128]{2,0,1:T(8,128)(2,1)S(1)} %get-tuple-element.146), channel_id=1, source_target_pairs={{32,0},{64,32},{96,64},{128,96},{160,128},{192,160},{224,192},{256... | collective-permute-start | bytes 36872 | tf_op jit(solution)/shard_map/ppermute | solution.py:20
  116.1 15.5 %collective-permute-start.31 = (bf16[75,128]{0,1:T(8,128)(2,1)S(1)}, bf16[75,128]{0,1:T(8,128)(2,1)S(1)}, u32[]{:S(2)}, u32[]{:S(2)}) collective-permute-start(bf16[75,128]{0,1:T(8,128)(2,1)S(1)} %get-tuple-element.126), channel_id=1, source_target_pairs={{0,1},{1,0},{2,3},{3,2},{4,5},{5,4},{6,7},{7,6},{8,9},{9,8},{10,11... | collective-permute-start | bytes 57608 | tf_op jit(solution)/shard_map/ppermute | solution.py:9
  121.4 13.9 %collective-permute-start.12 = (bf16[48,128]{1,0:T(8,128)(2,1)S(1)}, bf16[48,128]{1,0:T(8,128)(2,1)S(1)}, u32[]{:S(2)}, u32[]{:S(2)}) collective-permute-start(bf16[48,128]{1,0:T(8,128)(2,1)S(1)} %collective-permute-done.11), channel_id=1, source_target_pairs={{0,4},{1,5},{2,6},{3,7},{4,0},{5,1},{6,2},{7,3},{8,12},{9,13},{10,... | collective-permute-start | bytes 36872 | tf_op jit(solution)/shard_map/ppermute | solution.py:9
  124.2 24.2 %collective-permute-start.30 = (bf16[1,75,128]{1,2,0:T(8,128)(2,1)S(1)}, bf16[1,75,128]{1,2,0:T(8,128)(2,1)S(1)}, u32[]{:S(2)}, u32[]{:S(2)}) collective-permute-start(bf16[1,75,128]{1,2,0:T(8,128)(2,1)S(1)} %get-tuple-element.127), channel_id=1, source_target_pairs={{32,0},{64,32},{96,64},{128,96},{160,128},{192,160},{224,192},{256... | collective-permute-start | bytes 57608 | tf_op jit(solution)/shard_map/ppermute | solution.py:20
  125.5 22.9 %collective-permute-start.29 = (bf16[1,75,128]{1,2,0:T(8,128)(2,1)S(1)}, bf16[1,75,128]{1,2,0:T(8,128)(2,1)S(1)}, u32[]{:S(2)}, u32[]{:S(2)}) collective-permute-start(bf16[1,75,128]{1,2,0:T(8,128)(2,1)S(1)} %get-tuple-element.128), channel_id=1, source_target_pairs={{0,32},{32,64},{64,96},{96,128},{128,160},{160,192},{192,224},{224... | collective-permute-start | bytes 57608 | tf_op jit(solution)/shard_map/ppermute | solution.py:19
  131.6 12.3 %collective-permute-start.32 = (bf16[75,128]{0,1:T(8,128)(2,1)S(1)}, bf16[75,128]{0,1:T(8,128)(2,1)S(1)}, u32[]{:S(2)}, u32[]{:S(2)}) collective-permute-start(bf16[75,128]{0,1:T(8,128)(2,1)S(1)} %collective-permute-done.31), channel_id=1, source_target_pairs={{0,2},{1,3},{2,0},{3,1},{4,6},{5,7},{6,4},{7,5},{8,10},{9,11},{10,... | collective-permute-start | bytes 57608 | tf_op jit(solution)/shard_map/ppermute | solution.py:9
  135.3 10.5 %collective-permute-start.13 = (bf16[48,128]{1,0:T(8,128)(2,1)S(1)}, bf16[48,128]{1,0:T(8,128)(2,1)S(1)}, u32[]{:S(2)}, u32[]{:S(2)}) collective-permute-start(bf16[48,128]{1,0:T(8,128)(2,1)S(1)} %collective-permute-done.12), channel_id=1, source_target_pairs={{0,8},{1,9},{2,10},{3,11},{4,12},{5,13},{6,14},{7,15},{8,0},{9,1},... | collective-permute-start | bytes 36872 | tf_op jit(solution)/shard_map/ppermute | solution.py:9
  145.8 9.0 %collective-permute-start.14 = (bf16[48,128]{1,0:T(8,128)(2,1)S(1)}, bf16[48,128]{1,0:T(8,128)(2,1)S(1)}, u32[]{:S(2)}, u32[]{:S(2)}) collective-permute-start(bf16[48,128]{1,0:T(8,128)(2,1)S(1)} %collective-permute-done.13), channel_id=1, source_target_pairs={{0,16},{1,17},{2,18},{3,19},{4,20},{5,21},{6,22},{7,23},{8,24},{9,... | collective-permute-start | bytes 36872 | tf_op jit(solution)/shard_map/ppermute | solution.py:9
  149.4 17.9 %collective-permute-start.34 = (bf16[75,128]{0,1:T(8,128)(2,1)S(1)}, bf16[75,128]{0,1:T(8,128)(2,1)S(1)}, u32[]{:S(2)}, u32[]{:S(2)}) collective-permute-start(bf16[75,128]{0,1:T(8,128)(2,1)S(1)} %collective-permute-done.33), channel_id=1, source_target_pairs={{0,8},{1,9},{2,10},{3,11},{4,12},{5,13},{6,14},{7,15},{8,0},{9,1},... | collective-permute-start | bytes 57608 | tf_op jit(solution)/shard_map/ppermute | solution.py:9
  (19 other events, 113.1 us)
Sparse Core Ops, SparseCore 0:
  172.6 272.8 all-reduce.4
where the time goes:
time: 456 us; the launch traced here: 455 us
  waiting for transfers between devices  283 us (62%)
  starting transfers between devices  133 us (29%)
  between operations  15.3 us (3%)
  matrix products  13.4 us (3%)
  local copies, waits for them, and re-layouts  5.33 us (1%)
  other arithmetic  4.94 us (1%)
    psum x1, waiting for transfers between devices, body(): grad_w1, grad_w2 = lax.psum((term_w1, term_w2), ('lat', 'lon'))  271 us
    ppermute x20, starting transfers between devices, from_partner(): lax.ppermute(x, axis, [(i, i ^ 1 << bit) for i in range(lax.axis_size(axi...  79.5 us
    ppermute x8, starting transfers between devices, extended(): before = lax.ppermute(last, axis, up)  29.3 us
    ppermute x8, starting transfers between devices, extended(): after = lax.ppermute(leading, axis, down)  24.3 us
  transfers between devices with their start and end apart: 37, of which 11 were waited for; matrix products, arithmetic and copies ran while one was open for 3% of the time, Pallas kernels for 0%

commit v1 on v0

--- a/solution.py
+++ b/solution.py
@@ -139,7 +139,13 @@
     term_w1 = wgrad(grad_a, x_ext)
     grad_x_ext = tconv(grad_a, w1)
     dx = retract(grad_x_ext).astype(jnp.bfloat16)
-    grad_w1, grad_w2 = lax.psum((term_w1, term_w2), ("lat", "lon"))
+
+    def find_squares(net_axis, slab_in, mesh_dim):
+        high = lax.psum(slab_in, mesh_dim)
+        tall = lax.psum(high, net_axis)
+        return tall
+
+    grad_w1, grad_w2 = find_squares("lat", (term_w1, term_w2), "lon")
     cells = fields.shape[1] * fields.shape[2] * lax.axis_size("lat") * lax.axis_size("lon")
     factor = 1.0 / math.sqrt(cells)
     return (out_block, dx, grad_w1 * factor, grad_w2 * factor)

time: 456 us -> 587 us (1.29); the launches traced: 455 us -> 577 us
  waiting for transfers between devices: 283 us -> 404 us
    psum x1 -> x2, waiting for transfers between devices: 271 us -> 392 us  [the longest x1 262 us: find_squares(): high = lax.psum(slab_in, mesh_dim)]
  transfers between devices with their start and end apart: 37 -> 38, of which waited for: 11 -> 12; matrix products, arithmetic and copies ran while one was open for 3% -> 2% of each run, Pallas kernels for 0% -> 0%
where the time goes in v1:
time: 587 us; the launch traced here: 577 us
  waiting for transfers between devices  404 us (69%)
  starting transfers between devices  133 us (23%)
  between operations  15.3 us (3%)
  matrix products  13.4 us (2%)
  local copies, waits for them, and re-layouts  5.97 us (1%)
    psum x1, waiting for transfers between devices, find_squares(): high = lax.psum(slab_in, mesh_dim)  262 us
    psum x1, waiting for transfers between devices, find_squares(): tall = lax.psum(high, net_axis)  130 us
    ppermute x20, starting transfers between devices, from_partner(): lax.ppermute(x, axis, [(i, i ^ 1 << bit) for i in range(lax.axis_size(axi...  79.6 us
    ppermute x8, starting transfers between devices, extended(): before = lax.ppermute(last, axis, up)  29.3 us
    ppermute x8, starting transfers between devices, extended(): after = lax.ppermute(leading, axis, down)  24.3 us
  transfers between devices with their start and end apart: 38, of which 12 were waited for; matrix products, arithmetic and copies ran while one was open for 2% of the time, Pallas kernels for 0%

profile of v1, /device:TPU:1, one launch (start us, length us, event | category | flops | bytes accessed | tf_op | source)
XLA Modules:
  0.0 576.5 jit_solution(6585898775259117079)
XLA Ops:
  11.8 4.6 collective-permute-start.18
  16.4 6.1 %collective-permute-start.19 = (f32[1,48,10]{1,0,2:T(1,128)S(1)}, f32[1,48,10]{1,0,2:T(1,128)S(1)}, u32[]{:S(2)}, u32[]{:S(2)}) collective-permute-start(f32[1,48,10]{1,0,2:T(1,128)S(1)} %stack_squeeze.29), channel_id=1, source_target_pairs={{1,0},{2,1},{3,2},{4,3},{5,4},{6,5},{7,6},{8,7},{9,8},{10,9},{11,1... | collective-permute-start | bytes 5768 | tf_op jit(solution)/shard_map/ppermute | solution.py:20
  22.7 7.3 %collective-permute-start.1 = (bf16[75,128]{0,1:T(8,128)(2,1)S(1)}, bf16[75,128]{0,1:T(8,128)(2,1)S(1)}, u32[]{:S(2)}, u32[]{:S(2)}) collective-permute-start(bf16[75,128]{0,1:T(8,128)(2,1)S(1)} %bitcast.327), channel_id=1, source_target_pairs={{0,1},{1,0},{2,3},{3,2},{4,5},{5,4},{6,7},{7,6},{8,9},{9,8},{10,11... | collective-permute-start | bytes 57608 | tf_op jit(solution)/shard_map/ppermute | solution.py:9
  36.9 3.4 collective-permute-start.23
  43.5 4.3 collective-permute-start.24
  47.8 4.0 collective-permute-start.20
  55.4 2.8 collective-permute-start.25
  58.1 6.4 %collective-permute-start.4 = (bf16[75,128]{0,1:T(8,128)(2,1)S(1)}, bf16[75,128]{0,1:T(8,128)(2,1)S(1)}, u32[]{:S(2)}, u32[]{:S(2)}) collective-permute-start(bf16[75,128]{0,1:T(8,128)(2,1)S(1)} %collective-permute-done.3), channel_id=1, source_target_pairs={{0,8},{1,9},{2,10},{3,11},{4,12},{5,13},{6,14},{7,15},{8,0},{9,1},... | collective-permute-start | bytes 57608 | tf_op jit(solution)/shard_map/ppermute | solution.py:9
  66.9 4.8 collective-permute-start.5
  73.4 6.0 %collective-permute-start.8 = (bf16[75,10,1]{2,0,1:T(8,128)(2,1)S(1)}, bf16[75,10,1]{2,0,1:T(8,128)(2,1)S(1)}, u32[]{:S(2)}, u32[]{:S(2)}) collective-permute-start(bf16[75,10,1]{2,0,1:T(8,128)(2,1)S(1)} %get-tuple-element.136), channel_id=1, source_target_pairs={{1,0},{2,1},{3,2},{4,3},{5,4},{6,5},{7,6},{8,7},{9,8},{10,9},{11,1... | collective-permute-start | bytes 4508 | tf_op jit(solution)/shard_map/ppermute | solution.py:20
  79.5 3.1 collective-permute-start.7
  88.0 4.5 collective-permute-start.9
  92.5 7.7 %collective-permute-start.10 = (bf16[48,128]{1,0:T(8,128)(2,1)S(1)}, bf16[48,128]{1,0:T(8,128)(2,1)S(1)}, u32[]{:S(2)}, u32[]{:S(2)}) collective-permute-start(bf16[48,128]{1,0:T(8,128)(2,1)S(1)} %get-tuple-element.147), channel_id=1, source_target_pairs={{0,1},{1,0},{2,3},{3,2},{4,5},{5,4},{6,7},{7,6},{8,9},{9,8},{10,11... | collective-permute-start | bytes 36872 | tf_op jit(solution)/shard_map/ppermute | solution.py:9
  111.3 2.7 collective-permute-done.28
  116.1 5.3 collective-permute-start.31
  125.5 6.1 %collective-permute-start.29 = (bf16[1,75,128]{1,2,0:T(8,128)(2,1)S(1)}, bf16[1,75,128]{1,2,0:T(8,128)(2,1)S(1)}, u32[]{:S(2)}, u32[]{:S(2)}) collective-permute-start(bf16[1,75,128]{1,2,0:T(8,128)(2,1)S(1)} %get-tuple-element.130), channel_id=1, source_target_pairs={{0,32},{32,64},{64,96},{96,128},{128,160},{160,192},{192,224},{224... | collective-permute-start | bytes 57608 | tf_op jit(solution)/shard_map/ppermute | solution.py:19
  131.6 3.6 collective-permute-start.32
  135.3 8.4 %collective-permute-start.13 = (bf16[48,128]{1,0:T(8,128)(2,1)S(1)}, bf16[48,128]{1,0:T(8,128)(2,1)S(1)}, u32[]{:S(2)}, u32[]{:S(2)}) collective-permute-start(bf16[48,128]{1,0:T(8,128)(2,1)S(1)} %collective-permute-done.12), channel_id=1, source_target_pairs={{0,8},{1,9},{2,10},{3,11},{4,12},{5,13},{6,14},{7,15},{8,0},{9,1},... | collective-permute-start | bytes 36872 | tf_op jit(solution)/shard_map/ppermute | solution.py:9
  149.4 5.3 collective-permute-start.34
  155.0 4.4 collective-permute-start.17
  159.4 3.3 collective-permute-start.16
  168.1 4.1 collective-permute-start.35
  174.3 262.4 %all-reduce.7.cloned.1.call-done = (f32[9,48,75]{2,1,0:T(8,128)}, f32[9,48,48]{2,1,0:T(8,128)}) async-done(((f32[9,48,75]{2,1,0:T(8,128)}, f32[9,48,48]{2,1,0:T(8,128)}), (f32[9,48,75]{2,1,0:T(8,128)}, f32[9,48,48]{2,1,0:T(8,128)})) %all-reduce.7.cloned.1.call-update) | async-done | bytes 212560 | tf_op jit(solution)/shard_map/psum | solution.py:144
  437.7 129.6 %all-reduce.9.cloned.1.call-done = (f32[9,48,75]{2,1,0:T(8,128)}, f32[9,48,48]{2,1,0:T(8,128)}) async-done(((f32[9,48,75]{2,1,0:T(8,128)}, f32[9,48,48]{2,1,0:T(8,128)}), (f32[9,48,75]{2,1,0:T(8,128)}, f32[9,48,48]{2,1,0:T(8,128)})) %all-reduce.9.cloned.1.call-update) | async-done | bytes 212560 | tf_op jit(solution)/shard_map/psum | solution.py:145
  (170 shorter events, 61.0 us)
Async XLA Ops:
  7.2 429.5 %all-reduce.7.cloned.1.call-start = ((), (), s32[]{:S(2)}) async-start(), calls=%async_computation | async-start | bytes 884736 | tf_op jit(solution)/shard_map/psum | solution.py:144
  11.8 18.5 %collective-permute-start.18 = (f32[1,48,10]{1,0,2:T(1,128)S(1)}, f32[1,48,10]{1,0,2:T(1,128)S(1)}, u32[]{:S(2)}, u32[]{:S(2)}) collective-permute-start(f32[1,48,10]{1,0,2:T(1,128)S(1)} %stack_squeeze.28), channel_id=1, source_target_pairs={{0,1},{1,2},{2,3},{3,4},{4,5},{5,6},{6,7},{7,8},{8,9},{9,10},{10,1... | collective-permute-start | bytes 5768 | tf_op jit(solution)/shard_map/ppermute | solution.py:19
  16.4 13.7 %collective-permute-start.19 = (f32[1,48,10]{1,0,2:T(1,128)S(1)}, f32[1,48,10]{1,0,2:T(1,128)S(1)}, u32[]{:S(2)}, u32[]{:S(2)}) collective-permute-start(f32[1,48,10]{1,0,2:T(1,128)S(1)} %stack_squeeze.29), channel_id=1, source_target_pairs={{1,0},{2,1},{3,2},{4,3},{5,4},{6,5},{7,6},{8,7},{9,8},{10,9},{11,1... | collective-permute-start | bytes 5768 | tf_op jit(solution)/shard_map/ppermute | solution.py:20
  22.7 9.2 %collective-permute-start.1 = (bf16[75,128]{0,1:T(8,128)(2,1)S(1)}, bf16[75,128]{0,1:T(8,128)(2,1)S(1)}, u32[]{:S(2)}, u32[]{:S(2)}) collective-permute-start(bf16[75,128]{0,1:T(8,128)(2,1)S(1)} %bitcast.327), channel_id=1, source_target_pairs={{0,1},{1,0},{2,3},{3,2},{4,5},{5,4},{6,7},{7,6},{8,9},{9,8},{10,11... | collective-permute-start | bytes 57608 | tf_op jit(solution)/shard_map/ppermute | solution.py:9
  40.3 17.9 %collective-permute-start.3 = (bf16[75,128]{0,1:T(8,128)(2,1)S(1)}, bf16[75,128]{0,1:T(8,128)(2,1)S(1)}, u32[]{:S(2)}, u32[]{:S(2)}) collective-permute-start(bf16[75,128]{0,1:T(8,128)(2,1)S(1)} %collective-permute-done.2), channel_id=1, source_target_pairs={{0,4},{1,5},{2,6},{3,7},{4,0},{5,1},{6,2},{7,3},{8,12},{9,13},{10,... | collective-permute-start | bytes 57608 | tf_op jit(solution)/shard_map/ppermute | solution.py:9
  42.2 11.7 %collective-permute-start.21 = (bf16[1,48,128]{2,1,0:T(8,128)(2,1)S(1)}, bf16[1,48,128]{2,1,0:T(8,128)(2,1)S(1)}, u32[]{:S(2)}, u32[]{:S(2)}) collective-permute-start(bf16[1,48,128]{2,1,0:T(8,128)(2,1)S(1)} %get-tuple-element.132), channel_id=1, source_target_pairs={{32,0},{64,32},{96,64},{128,96},{160,128},{192,160},{224,192},{256... | collective-permute-start | bytes 36872 | tf_op jit(solution)/shard_map/ppermute | solution.py:20
  43.5 11.8 %collective-permute-start.24 = (bf16[48,128]{1,0:T(8,128)(2,1)S(1)}, bf16[48,128]{1,0:T(8,128)(2,1)S(1)}, u32[]{:S(2)}, u32[]{:S(2)}) collective-permute-start(bf16[48,128]{1,0:T(8,128)(2,1)S(1)} %collective-permute-done.23), channel_id=1, source_target_pairs={{0,4},{1,5},{2,6},{3,7},{4,0},{5,1},{6,2},{7,3},{8,12},{9,13},{10,... | collective-permute-start | bytes 36872 | tf_op jit(solution)/shard_map/ppermute | solution.py:9
  47.8 16.8 %collective-permute-start.20 = (bf16[1,48,128]{2,1,0:T(8,128)(2,1)S(1)}, bf16[1,48,128]{2,1,0:T(8,128)(2,1)S(1)}, u32[]{:S(2)}, u32[]{:S(2)}) collective-permute-start(bf16[1,48,128]{2,1,0:T(8,128)(2,1)S(1)} %get-tuple-element.133), channel_id=1, source_target_pairs={{0,32},{32,64},{64,96},{96,128},{128,160},{160,192},{192,224},{224... | collective-permute-start | bytes 36872 | tf_op jit(solution)/shard_map/ppermute | solution.py:19
  51.8 12.8 %collective-permute-start = (bf16[75,1,128]{0,2,1:T(8,128)(2,1)S(1)}, bf16[75,1,128]{0,2,1:T(8,128)(2,1)S(1)}, u32[]{:S(2)}, u32[]{:S(2)}) collective-permute-start(bf16[75,1,128]{0,2,1:T(8,128)(2,1)S(1)} %copy.200), channel_id=1, source_target_pairs={{0,32},{32,64},{64,96},{96,128},{128,160},{160,192},{192,224},{224... | collective-permute-start | bytes 57608 | tf_op jit(solution)/shard_map/ppermute | solution.py:19
  53.9 19.2 %collective-permute-start.6 = (bf16[75,1,128]{0,2,1:T(8,128)(2,1)S(1)}, bf16[75,1,128]{0,2,1:T(8,128)(2,1)S(1)}, u32[]{:S(2)}, u32[]{:S(2)}) collective-permute-start(bf16[75,1,128]{0,2,1:T(8,128)(2,1)S(1)} %copy.201), channel_id=1, source_target_pairs={{32,0},{64,32},{96,64},{128,96},{160,128},{192,160},{224,192},{256... | collective-permute-start | bytes 57608 | tf_op jit(solution)/shard_map/ppermute | solution.py:20
  55.4 9.4 %collective-permute-start.25 = (bf16[48,128]{1,0:T(8,128)(2,1)S(1)}, bf16[48,128]{1,0:T(8,128)(2,1)S(1)}, u32[]{:S(2)}, u32[]{:S(2)}) collective-permute-start(bf16[48,128]{1,0:T(8,128)(2,1)S(1)} %collective-permute-done.24), channel_id=1, source_target_pairs={{0,8},{1,9},{2,10},{3,11},{4,12},{5,13},{6,14},{7,15},{8,0},{9,1},... | collective-permute-start | bytes 36872 | tf_op jit(solution)/shard_map/ppermute | solution.py:9
  73.4 10.7 %collective-permute-start.8 = (bf16[75,10,1]{2,0,1:T(8,128)(2,1)S(1)}, bf16[75,10,1]{2,0,1:T(8,128)(2,1)S(1)}, u32[]{:S(2)}, u32[]{:S(2)}) collective-permute-start(bf16[75,10,1]{2,0,1:T(8,128)(2,1)S(1)} %get-tuple-element.136), channel_id=1, source_target_pairs={{1,0},{2,1},{3,2},{4,3},{5,4},{6,5},{7,6},{8,7},{9,8},{10,9},{11,1... | collective-permute-start | bytes 4508 | tf_op jit(solution)/shard_map/ppermute | solution.py:20
  88.0 37.5 %collective-permute-start.9 = (bf16[48,1,128]{2,0,1:T(8,128)(2,1)S(1)}, bf16[48,1,128]{2,0,1:T(8,128)(2,1)S(1)}, u32[]{:S(2)}, u32[]{:S(2)}) collective-permute-start(bf16[48,1,128]{2,0,1:T(8,128)(2,1)S(1)} %get-tuple-element.146), channel_id=1, source_target_pairs={{0,32},{32,64},{64,96},{96,128},{128,160},{160,192},{192,224},{224... | collective-permute-start | bytes 36872 | tf_op jit(solution)/shard_map/ppermute | solution.py:19
  92.5 21.6 %collective-permute-start.10 = (bf16[48,128]{1,0:T(8,128)(2,1)S(1)}, bf16[48,128]{1,0:T(8,128)(2,1)S(1)}, u32[]{:S(2)}, u32[]{:S(2)}) collective-permute-start(bf16[48,128]{1,0:T(8,128)(2,1)S(1)} %get-tuple-element.147), channel_id=1, source_target_pairs={{0,1},{1,0},{2,3},{3,2},{4,5},{5,4},{6,7},{7,6},{8,9},{9,8},{10,11... | collective-permute-start | bytes 36872 | tf_op jit(solution)/shard_map/ppermute | solution.py:9
  100.2 54.6 %collective-permute-start.15 = (bf16[48,1,128]{2,0,1:T(8,128)(2,1)S(1)}, bf16[48,1,128]{2,0,1:T(8,128)(2,1)S(1)}, u32[]{:S(2)}, u32[]{:S(2)}) collective-permute-start(bf16[48,1,128]{2,0,1:T(8,128)(2,1)S(1)} %get-tuple-element.148), channel_id=1, source_target_pairs={{32,0},{64,32},{96,64},{128,96},{160,128},{192,160},{224,192},{256... | collective-permute-start | bytes 36872 | tf_op jit(solution)/shard_map/ppermute | solution.py:20
  116.1 15.5 %collective-permute-start.31 = (bf16[75,128]{0,1:T(8,128)(2,1)S(1)}, bf16[75,128]{0,1:T(8,128)(2,1)S(1)}, u32[]{:S(2)}, u32[]{:S(2)}) collective-permute-start(bf16[75,128]{0,1:T(8,128)(2,1)S(1)} %get-tuple-element.128), channel_id=1, source_target_pairs={{0,1},{1,0},{2,3},{3,2},{4,5},{5,4},{6,7},{7,6},{8,9},{9,8},{10,11... | collective-permute-start | bytes 57608 | tf_op jit(solution)/shard_map/ppermute | solution.py:9
  121.4 13.9 %collective-permute-start.12 = (bf16[48,128]{1,0:T(8,128)(2,1)S(1)}, bf16[48,128]{1,0:T(8,128)(2,1)S(1)}, u32[]{:S(2)}, u32[]{:S(2)}) collective-permute-start(bf16[48,128]{1,0:T(8,128)(2,1)S(1)} %collective-permute-done.11), channel_id=1, source_target_pairs={{0,4},{1,5},{2,6},{3,7},{4,0},{5,1},{6,2},{7,3},{8,12},{9,13},{10,... | collective-permute-start | bytes 36872 | tf_op jit(solution)/shard_map/ppermute | solution.py:9
  124.2 24.2 %collective-permute-start.30 = (bf16[1,75,128]{1,2,0:T(8,128)(2,1)S(1)}, bf16[1,75,128]{1,2,0:T(8,128)(2,1)S(1)}, u32[]{:S(2)}, u32[]{:S(2)}) collective-permute-start(bf16[1,75,128]{1,2,0:T(8,128)(2,1)S(1)} %get-tuple-element.129), channel_id=1, source_target_pairs={{32,0},{64,32},{96,64},{128,96},{160,128},{192,160},{224,192},{256... | collective-permute-start | bytes 57608 | tf_op jit(solution)/shard_map/ppermute | solution.py:20
  125.5 22.9 %collective-permute-start.29 = (bf16[1,75,128]{1,2,0:T(8,128)(2,1)S(1)}, bf16[1,75,128]{1,2,0:T(8,128)(2,1)S(1)}, u32[]{:S(2)}, u32[]{:S(2)}) collective-permute-start(bf16[1,75,128]{1,2,0:T(8,128)(2,1)S(1)} %get-tuple-element.130), channel_id=1, source_target_pairs={{0,32},{32,64},{64,96},{96,128},{128,160},{160,192},{192,224},{224... | collective-permute-start | bytes 57608 | tf_op jit(solution)/shard_map/ppermute | solution.py:19
  131.6 12.2 %collective-permute-start.32 = (bf16[75,128]{0,1:T(8,128)(2,1)S(1)}, bf16[75,128]{0,1:T(8,128)(2,1)S(1)}, u32[]{:S(2)}, u32[]{:S(2)}) collective-permute-start(bf16[75,128]{0,1:T(8,128)(2,1)S(1)} %collective-permute-done.31), channel_id=1, source_target_pairs={{0,2},{1,3},{2,0},{3,1},{4,6},{5,7},{6,4},{7,5},{8,10},{9,11},{10,... | collective-permute-start | bytes 57608 | tf_op jit(solution)/shard_map/ppermute | solution.py:9
  135.3 10.5 %collective-permute-start.13 = (bf16[48,128]{1,0:T(8,128)(2,1)S(1)}, bf16[48,128]{1,0:T(8,128)(2,1)S(1)}, u32[]{:S(2)}, u32[]{:S(2)}) collective-permute-start(bf16[48,128]{1,0:T(8,128)(2,1)S(1)} %collective-permute-done.12), channel_id=1, source_target_pairs={{0,8},{1,9},{2,10},{3,11},{4,12},{5,13},{6,14},{7,15},{8,0},{9,1},... | collective-permute-start | bytes 36872 | tf_op jit(solution)/shard_map/ppermute | solution.py:9
  145.8 9.0 %collective-permute-start.14 = (bf16[48,128]{1,0:T(8,128)(2,1)S(1)}, bf16[48,128]{1,0:T(8,128)(2,1)S(1)}, u32[]{:S(2)}, u32[]{:S(2)}) collective-permute-start(bf16[48,128]{1,0:T(8,128)(2,1)S(1)} %collective-permute-done.13), channel_id=1, source_target_pairs={{0,16},{1,17},{2,18},{3,19},{4,20},{5,21},{6,22},{7,23},{8,24},{9,... | collective-permute-start | bytes 36872 | tf_op jit(solution)/shard_map/ppermute | solution.py:9
  149.4 18.7 %collective-permute-start.34 = (bf16[75,128]{0,1:T(8,128)(2,1)S(1)}, bf16[75,128]{0,1:T(8,128)(2,1)S(1)}, u32[]{:S(2)}, u32[]{:S(2)}) collective-permute-start(bf16[75,128]{0,1:T(8,128)(2,1)S(1)} %collective-permute-done.33), channel_id=1, source_target_pairs={{0,8},{1,9},{2,10},{3,11},{4,12},{5,13},{6,14},{7,15},{8,0},{9,1},... | collective-permute-start | bytes 57608 | tf_op jit(solution)/shard_map/ppermute | solution.py:9
  167.6 399.7 %all-reduce.9.cloned.1.call-start = ((), (), s32[]{:S(2)}) async-start(), calls=%async_computation.1 | async-start | bytes 884736 | tf_op jit(solution)/shard_map/psum | solution.py:145
  (20 other events, 121.9 us)
Sparse Core Ops, SparseCore 0:
  167.8 268.9 all-reduce.6
  440.0 127.2 all-reduce.8
